TPU v7x, 32 devices: a whole 2x2x4 slice. The times are simulated.
32 devices in a mesh: dp: 16 (over z, x, core), src: 2 (over y).
Axes of the slice: x: 2, y: 2, z: 4, core: 2. Of those that a mesh axis runs over, the one named last changes fastest.
Arguments:
- inputs: float32 [96, 256, 512], P(('dp', 'src')), may hold values from -6 to 6
- memory: float32 [96, 256, 512], P('dp', 'src'), may hold values from -6 to 6
- timesteps: int32 [96], P(('dp', 'src')), may hold values from 0 to 49
- mask_flags: int32 [96, 256], P(('dp', 'src')), may hold values from 0 to 1, as said below
- time_table: float32 [50, 512], replicated, may hold values from -3 to 3
- mask_vector: float32 [512], replicated, may hold values from -6 to 6
- first_gain: float32 [512], replicated, may hold values from 0.5 to 1.5
- first_bias: float32 [512], replicated, may hold values from -2 to 2
- self_qkv: float32 [512, 1536], replicated, may hold values from -0.25 to 0.25
- self_out: float32 [512, 512], replicated, may hold values from -1 to 1
- cross_query: float32 [512, 512], replicated, may hold values from -0.25 to 0.25
- cross_kv: float32 [512, 1024], replicated, may hold values from -0.25 to 0.25
- cross_out: float32 [512, 512], replicated, may hold values from -1 to 1
- second_gain: float32 [512], replicated, may hold values from 0.5 to 1.5
- second_bias: float32 [512], replicated, may hold values from -2 to 2
- expand_weight: float32 [512, 2048], replicated, may hold values from -0.25 to 0.25
- reduce_weight: float32 [2048, 512], replicated, may hold values from -0.125 to 0.125
- cotangent: float32 [96, 256, 512], P(('dp', 'src')), may hold values from -6 to 6
Outputs:
- output: float32 [96, 256, 512], P(('dp', 'src'))
- input_grad: float32 [96, 256, 512], P(('dp', 'src'))
- memory_grad: float32 [96, 256, 512], P('dp', 'src')
- time_grad: float32 [50, 512], replicated
- mask_grad: float32 [512], replicated
- first_gain_grad: float32 [512], replicated
- first_bias_grad: float32 [512], replicated
- self_qkv_grad: float32 [512, 1536], replicated
- self_out_grad: float32 [512, 512], replicated
- cross_query_grad: float32 [512, 512], replicated
- cross_kv_grad: float32 [512, 1024], replicated
- cross_out_grad: float32 [512, 512], replicated
- second_gain_grad: float32 [512], replicated
- second_bias_grad: float32 [512], replicated
- expand_grad: float32 [512, 2048], replicated
- reduce_grad: float32 [2048, 512], replicated
Inputs may be any that keep to these rules, and one draw needn't show every extreme that they name: `mask_flags`: each item marks between 1 and 256 of its tokens.
All inputs are finite; a program needn't handle non-finite values.
Results may differ from a plain program's by a relative error of at most 0.0003.
Values sent between devices are 32-bit elements; how exact they have to be, the bound alone decides.
No kernel may reach another device: no remote copies, remote signals or barrier semaphores. Data moves between devices by JAX's collectives and lax.ppermute only.
A program may use at most 192 MiB of HBM per device.

v0:
```python
import jax
import jax.numpy as jnp
from jax import lax
from jax.sharding import PartitionSpec as P

HEADS = 8


precise = lax.Precision.HIGHEST
epsilon = 1e-05


def combined_all(x, axis, combine):
    everything = jax.tree.map(lambda part: lax.all_gather(part, axis), x)
    initial = jax.tree.map(lambda part: part[0], everything)

    def turn(k, so_far):
        return combine(so_far, jax.tree.map(lambda part: part[k], everything))

    return lax.fori_loop(1, lax.axis_size(axis), turn, initial)


def norm_forward(values, norm_gain, norm_bias):
    centred = values - jnp.mean(values, -1, keepdims=True)
    inverse = lax.rsqrt(jnp.mean(centred * centred, -1, keepdims=True) + epsilon)
    normed = centred * inverse
    return (normed * norm_gain + norm_bias, normed, inverse)


def norm_backward(grad_out, normed, inverse, norm_gain):
    scaled = grad_out * norm_gain
    grad_in = inverse * (
        scaled
        - jnp.mean(scaled, -1, keepdims=True)
        - normed * jnp.mean(scaled * normed, -1, keepdims=True)
    )
    return (grad_in, jnp.sum(grad_out * normed, (0, 1)), jnp.sum(grad_out, (0, 1)))


def heads_of(values):
    return values.reshape(values.shape[0], values.shape[1], HEADS, values.shape[2] // HEADS)


def joined(values):
    return values.reshape(values.shape[0], values.shape[1], values.shape[2] * values.shape[3])


def scores_of(query_heads, key_heads):
    return jnp.einsum(
        "bqhe,bkhe->bhqk", query_heads, key_heads, precision=precise
    ) * query_heads.shape[-1] ** (-0.5)


def attend_stats(query_heads, key_heads, value_heads):
    scores = scores_of(query_heads, key_heads)
    highest = jnp.max(scores, -1)
    exponent = jnp.exp(scores - highest[..., None])
    totals = jnp.sum(exponent, -1)
    summed = jnp.einsum("bhqk,bkhe->bqhe", exponent, value_heads, precision=precise)
    return (summed, jnp.transpose(highest, (0, 2, 1)), jnp.transpose(totals, (0, 2, 1)))


def combine(earlier, later):
    earlier_sum, earlier_peak, earlier_total = earlier
    later_sum, later_peak, later_total = later
    highest = jnp.maximum(earlier_peak, later_peak)
    earlier_scale = jnp.exp(earlier_peak - highest)
    later_scale = jnp.exp(later_peak - highest)
    totals = earlier_total * earlier_scale + later_total * later_scale
    summed = earlier_sum * earlier_scale[..., None] + later_sum * later_scale[..., None]
    return (summed, highest, totals)


def attend_grads(query_heads, key_heads, value_heads, logsum, grad_out, attended):
    row_dots = jnp.sum(grad_out * attended, -1)
    weights = jnp.exp(
        scores_of(query_heads, key_heads) - jnp.transpose(logsum, (0, 2, 1))[..., None]
    )
    grad_values = jnp.einsum("bhqk,bqhe->bkhe", weights, grad_out, precision=precise)
    grad_weights = jnp.einsum("bqhe,bkhe->bhqk", grad_out, value_heads, precision=precise)
    grad_scores = (
        weights
        * (grad_weights - jnp.transpose(row_dots, (0, 2, 1))[..., None])
        * query_heads.shape[-1] ** (-0.5)
    )
    grad_queries = jnp.einsum("bhqk,bkhe->bqhe", grad_scores, key_heads, precision=precise)
    grad_keys = jnp.einsum("bhqk,bqhe->bkhe", grad_scores, query_heads, precision=precise)
    return (grad_queries, grad_keys, grad_values)


def smooth(values):
    return jax.nn.gelu(values, approximate=False)


def weight_grad(left, right):
    return jnp.einsum("bld,ble->de", left, right, precision=precise)


def shards(
    inputs,
    memory,
    timesteps,
    mask_flags,
    time_table,
    mask_vector,
    first_gain,
    first_bias,
    self_qkv,
    self_out,
    cross_query,
    cross_kv,
    cross_out,
    second_gain,
    second_bias,
    expand_weight,
    reduce_weight,
    cotangent,
):
    items = inputs.shape[0]
    width = inputs.shape[2]
    chosen = mask_flags.astype(jnp.float32)[..., None]
    onehot = (
        timesteps[:, None] == jnp.arange(time_table.shape[0], dtype=jnp.int32)[None, :]
    ).astype(jnp.float32)
    start = (
        inputs * (1.0 - chosen)
        + chosen * mask_vector
        + jnp.dot(onehot, time_table, precision=precise)[:, None, :]
    )
    normed_one, first_normed, first_inverse = norm_forward(start, first_gain, first_bias)
    packed = jnp.dot(normed_one, self_qkv, precision=precise)
    self_queries = heads_of(packed[..., :width])
    self_keys = heads_of(packed[..., width : 2 * width])
    self_values = heads_of(packed[..., 2 * width :])
    summed, highest, totals = attend_stats(self_queries, self_keys, self_values)
    self_attended = summed / totals[..., None]
    self_logsum = highest + jnp.log(totals)
    self_flat = joined(self_attended)
    middle = start + jnp.dot(self_flat, self_out, precision=precise)
    query_heads = heads_of(jnp.dot(middle, cross_query, precision=precise))
    memory_pairs = jnp.dot(memory, cross_kv, precision=precise)
    group_queries = lax.all_gather(query_heads, "src", axis=0, tiled=True)
    memory_keys = heads_of(memory_pairs[..., :width])
    memory_values = heads_of(memory_pairs[..., width:])
    summed, highest, totals = combined_all(
        attend_stats(group_queries, memory_keys, memory_values), "src", combine
    )
    group_attended = summed / totals[..., None]
    group_logsum = highest + jnp.log(totals)
    cross_attended = lax.dynamic_slice_in_dim(
        group_attended, lax.axis_index("src") * items, items, 0
    )
    cross_flat = joined(cross_attended)
    after_cross = middle + jnp.dot(cross_flat, cross_out, precision=precise)
    normed_two, second_normed, second_inverse = norm_forward(after_cross, second_gain, second_bias)
    pre_active = jnp.dot(normed_two, expand_weight, precision=precise)
    active, active_pull = jax.vjp(smooth, pre_active)
    output = after_cross + jnp.dot(active, reduce_weight, precision=precise)
    reduce_g = weight_grad(active, cotangent)
    grad_pre = active_pull(jnp.dot(cotangent, reduce_weight.T, precision=precise))[0]
    expand_g = weight_grad(normed_two, grad_pre)
    grad_normed_two = jnp.dot(grad_pre, expand_weight.T, precision=precise)
    grad_after, second_gain_g, second_bias_g = norm_backward(
        grad_normed_two, second_normed, second_inverse, second_gain
    )
    grad_after = grad_after + cotangent
    cross_out_g = weight_grad(cross_flat, grad_after)
    grad_cross = heads_of(jnp.dot(grad_after, cross_out.T, precision=precise))
    group_grads = lax.all_gather(grad_cross, "src", axis=0, tiled=True)
    part_queries, grad_keys, grad_values = attend_grads(
        group_queries, memory_keys, memory_values, group_logsum, group_grads, group_attended
    )
    grad_query_heads = lax.psum_scatter(part_queries, "src", scatter_dimension=0, tiled=True)
    grad_pairs = jnp.concatenate([joined(grad_keys), joined(grad_values)], -1)
    cross_kv_g = weight_grad(memory, grad_pairs)
    memory_grad = jnp.dot(grad_pairs, cross_kv.T, precision=precise)
    grad_query_flat = joined(grad_query_heads)
    cross_query_g = weight_grad(middle, grad_query_flat)
    grad_middle = grad_after + jnp.dot(grad_query_flat, cross_query.T, precision=precise)
    self_out_g = weight_grad(self_flat, grad_middle)
    grad_self = heads_of(jnp.dot(grad_middle, self_out.T, precision=precise))
    grad_self_queries, grad_self_keys, grad_self_values = attend_grads(
        self_queries, self_keys, self_values, self_logsum, grad_self, self_attended
    )
    grad_packed = jnp.concatenate(
        [joined(grad_self_queries), joined(grad_self_keys), joined(grad_self_values)], -1
    )
    self_qkv_g = weight_grad(normed_one, grad_packed)
    grad_normed_one = jnp.dot(grad_packed, self_qkv.T, precision=precise)
    grad_start, first_gain_g, first_bias_g = norm_backward(
        grad_normed_one, first_normed, first_inverse, first_gain
    )
    grad_start = grad_start + grad_middle
    input_grad = grad_start * (1.0 - chosen)
    mask_g = jnp.sum(grad_start * chosen, (0, 1))
    time_g = jnp.dot(onehot.T, jnp.sum(grad_start, 1), precision=precise)
    (
        time_g,
        mask_g,
        first_gain_g,
        first_bias_g,
        self_qkv_g,
        self_out_g,
        cross_query_g,
        cross_kv_g,
        cross_out_g,
        second_gain_g,
        second_bias_g,
        expand_g,
        reduce_g,
    ) = lax.psum(
        (
            time_g,
            mask_g,
            first_gain_g,
            first_bias_g,
            self_qkv_g,
            self_out_g,
            cross_query_g,
            cross_kv_g,
            cross_out_g,
            second_gain_g,
            second_bias_g,
            expand_g,
            reduce_g,
        ),
        ("dp", "src"),
    )
    return (
        output,
        input_grad,
        memory_grad,
        time_g,
        mask_g,
        first_gain_g,
        first_bias_g,
        self_qkv_g,
        self_out_g,
        cross_query_g,
        cross_kv_g,
        cross_out_g,
        second_gain_g,
        second_bias_g,
        expand_g,
        reduce_g,
    )


def solution(mesh):
    placed = (
        P(("dp", "src"), None, None),
        P("dp", "src", None),
        P(("dp", "src")),
        P(("dp", "src"), None),
        P(),
        P(),
        P(),
        P(),
        P(),
        P(),
        P(),
        P(),
        P(),
        P(),
        P(),
        P(),
        P(),
        P(("dp", "src"), None, None),
    )
    return jax.shard_map(
        shards,
        mesh=mesh,
        in_specs=placed,
        out_specs=(
            P(("dp", "src"), None, None),
            P(("dp", "src"), None, None),
            P("dp", "src", None),
            P(),
            P(),
            P(),
            P(),
            P(),
            P(),
            P(),
            P(),
            P(),
            P(),
            P(),
            P(),
            P(),
        ),
        check_vma=False,
    )
```

profile of v0, /device:TPU:0, one launch (start us, length us, event | category | flops | bytes accessed | tf_op | source)
XLA Modules:
  0.0 801.5 jit_solution(11545596366734159966)
XLA Ops:
  13.6 8.0 %fusion.30 = f32[3,256,1536]{2,1,0:T(8,128)S(1)} fusion(f32[512,1536]{1,0:T(8,128)S(1)} %copy-done, f32[512]{0:T(512)S(1)} %copy-done.56, f32[512]{0:T(512)S(1)} %copy-done.53, f32[3,256]{1,0:T(4,128)S(1)} %add_rsqrt_fusion.1, f32[3,256]{1,0:T(4,128)S(1)} %broadcast_multiply_fusion.6, f32[3,256,512]{2,1,0:T(8,128)S(1)} %copy-done.9, ...), kind=kOutput, calls=%fused_computation.61 | convolution fusion | flops 7250903040 | bytes 9461760 | tf_op jit(solution)/shard_map/dot_general | solution.py:131
  21.6 2.3 fusion.97
  23.9 3.1 copy.140
  27.0 3.0 copy.139
  30.0 3.0 copy.138
  33.0 7.8 multiply_reduce_fusion.1
  43.4 4.8 bitcast_divide_fusion
  48.3 3.1 convolution_add_fusion.2
  51.4 4.3 fusion.59
  55.8 7.4 fusion.45
  63.2 2.0 fusion.98
  65.2 3.2 copy.145
  68.4 3.2 copy.143
  71.6 31.9 %all-gather.7.cloned.1.call-done = f32[6,256,8,64]{1,3,2,0:T(8,128)} async-done(((f32[3,256,8,64]{1,3,2,0:T(8,128)}), f32[6,256,8,64]{1,3,2,0:T(8,128)}) %all-gather.7.cloned.1.call-update) | async-done | bytes 3145744 | tf_op jit(solution)/shard_map/all_gather | solution.py:142
  103.5 8.1 %multiply_reduce_fusion = (f32[6,8,256]{2,1,0:T(8,128)S(1)}, f32[6,8,256,128]{2,3,1,0:T(8,128)S(1)}) fusion(f32[6,256,8,64]{1,3,2,0:T(8,128)} %all-gather.7.cloned.1.call-done, f32[6,128,8,64]{1,3,2,0:T(8,128)} %bitcast.165), kind=kOutput, calls=%fused_computation.37 | convolution fusion | flops 1211092992 | bytes 11059200 | tf_op jit(solution)/shard_map/bqhe,bkhe->bhqk/dot_general | solution.py:49
  111.6 2.6 copy-done.1
  114.2 6.1 fusion.47
  120.5 4.0 fusion.8
  124.5 4.8 all-gather.2
  129.3 5.8 all-gather.1
  135.1 66.4 %all-gather.11.cloned.1.call-done = f32[12,256,8,64]{1,3,2,0:T(8,128)} async-done(((f32[6,256,8,64]{1,3,2,0:T(8,128)}), f32[12,256,8,64]{1,3,2,0:T(8,128)}) %all-gather.11.cloned.1.call-update) | async-done | bytes 6291472 | tf_op jit(solution)/shard_map/all_gather | solution.py:14
  201.5 3.9 fusion.28
  207.6 2.8 fusion.99
  210.9 13.5 %fusion.50 = (u8[256,2048]{1,0:T(8,128)(4,1)S(1)}, u8[256,2048]{1,0:T(8,128)(4,1)S(1)}, u8[256,2048]{1,0:T(8,128)(4,1)S(1)}, f32[3,256,2048]{2,1,0:T(8,128)S(1)}) fusion(f32[512,2048]{1,0:T(8,128)S(1)} %copy-done.36, f32[3,256,512]{2,1,0:T(8,128)S(1)} %get-tuple-element.145, f32[512]{0:T(512)S(1)} %copy-done.55, f32[512]{0:T(512)S(1)} %copy-done.52, ...), kind=kOutput, calls=%fused_computation.95 | convolution fusion | flops 9695133696 | bytes 13641728 | tf_op jit(solution)/shard_map/dot_general | solution.py:156
  224.4 13.7 %fusion = f32[3,256,2048]{2,1,0:T(8,128)S(1)} fusion(f32[3,256,2048]{2,1,0:T(8,128)S(1)} %get-tuple-element.146, u8[256,2048]{1,0:T(8,128)(4,1)S(1)} %get-tuple-element.105, u8[256,2048]{1,0:T(8,128)(4,1)S(1)} %get-tuple-element.106, u8[256,2048]{1,0:T(8,128)(4,1)S(1)} %get-tuple-element.104), kind=kLoop, calls=%fused_computation.1 | loop fusion | flops 108527616 | bytes 14155776 | tf_op jit(solution)/shard_map/jvp()/erfc | solution.py:92
  238.2 15.7 %multiply_add_fusion = f32[3,256,2048]{2,1,0:T(8,128)S(1)} fusion(f32[3,256,2048]{2,1,0:T(8,128)S(1)} %fusion, f32[3,256,2048]{2,1,0:T(8,128)S(1)} %get-tuple-element.146, f32[3,256,512]{2,1,0:T(8,128)S(1)} %copy-done.31, f32[2048,512]{1,0:T(8,128)} %param.34), kind=kOutput, calls=%fused_computation.12 | convolution fusion | flops 9684123648 | bytes 24641536 | tf_op jit(solution)/shard_map/dot_general | solution.py:160
  253.9 15.4 %multiply_reduce_fusion.3 = (f32[512]{0:T(512)S(1)}, f32[3,256]{1,0:T(4,128)S(1)}, f32[3,256]{1,0:T(4,128)S(1)}, f32[512]{0:T(512)S(1)}, f32[3,256,512]{2,1,0:T(8,128)S(1)}) fusion(f32[3,256,512]{2,1,0:T(8,128)S(1)} %get-tuple-element.145, f32[3,256]{1,0:T(4,128)S(1)} %add_rsqrt_fusion, f32[3,256]{1,0:T(4,128)S(1)} %broadcast_multiply_fusion.5, ...), kind=kOutput, calls=%fused_computation.81 | convolution fusion | flops 9667213312 | bytes 13649920 | tf_op jit(solution)/shard_map/dot_general | solution.py:162
  269.9 3.9 fusion.55
  273.8 45.0 %all-gather.9.cloned.1.call-done = f32[6,256,8,64]{1,3,2,0:T(8,128)} async-done(((f32[3,256,8,64]{1,3,2,0:T(8,128)}), f32[6,256,8,64]{1,3,2,0:T(8,128)}) %all-gather.9.cloned.1.call-update) | async-done | bytes 3145744 | tf_op jit(solution)/shard_map/all_gather | solution.py:169
  318.9 5.5 multiply_reduce_fusion.2
  324.5 9.1 %multiply_multiply_fusion.1 = f32[6,8,256,128]{2,3,1,0:T(8,128)S(1)} fusion(f32[6,8,256,128]{2,3,1,0:T(8,128)} %copy-done.1, f32[6,8,256]{2,1,0:T(8,128)S(1)} %bitcast.180, f32[6,8,256]{2,1,0:T(8,128)S(1)} %get-tuple-element.131, f32[6,256,8,64]{1,3,2,0:T(8,128)S(1)} %copy-done.8, f32[6,128,8,64]{1,3,2,0:T(8,128)S(1)} %bitcast.158), kind=kOutput, calls=%fused_computation.10 | convolution fusion | flops 1215823872 | bytes 17399808 | tf_op jit(solution)/shard_map/bqhe,bkhe->bhqk/dot_general | solution.py:80
  333.6 2.7 copy-done.5
  336.3 5.4 convolution_bitcast_fusion.2
  341.9 5.7 convolution_bitcast_fusion.3
  347.6 14.9 %convolution_bitcast_fusion.1 = f32[512,2048]{1,0:T(8,128)} fusion(f32[3,256,2048]{2,1,0:T(8,128)} %copy-done.30, f32[3,256,512]{2,1,0:T(8,128)S(1)} %copy-done.7, f32[512]{0:T(512)S(1)} %copy-done.55, f32[512]{0:T(512)S(1)} %copy-done.52, f32[3,256]{1,0:T(4,128)S(1)} %add_rsqrt_fusion, f32[3,256]{1,0:T(4,128)S(1)} %broadcast_multiply_fusion.5), kind=kOutput, calls=%fused_computation.54 | convolution fusion | flops 9665249280 | bytes 12068864 | tf_op jit(solution)/shard_map/bld,ble->de/dot_general | solution.py:96
  362.6 12.0 %convolution_bitcast_fusion = f32[2048,512]{1,0:T(8,128)} fusion(f32[3,256,512]{2,1,0:T(8,128)S(1)} %copy-done.32, f32[3,256,2048]{2,1,0:T(8,128)S(1)} %bitcast.150, f32[3,256,2048]{2,1,0:T(8,128)S(1)} %bitcast.148), kind=kOutput, calls=%fused_computation.53 | convolution fusion | flops 9666822144 | bytes 18350080 | tf_op jit(solution)/shard_map/bld,ble->de/dot_general | solution.py:96
  374.6 7.8 fusion.102
  382.4 3.0 copy.162
  385.5 12.2 %fusion.11 = f32[6,8,64,128]{3,2,1,0:T(8,128)} fusion(f32[6,256,8,64]{1,3,2,0:T(8,128)} %all-gather.9.cloned.1.call-done, f32[6,8,256,128]{2,3,1,0:T(8,128)} %copy-done.1, f32[6,8,256]{2,1,0:T(8,128)S(1)} %get-tuple-element.131), kind=kOutput, calls=%fused_computation.34 | convolution fusion | flops 1211105280 | bytes 11059200 | tf_op jit(solution)/shard_map/bhqk,bqhe->bkhe/dot_general | solution.py:79
  397.7 3.1 copy.163
  400.8 8.9 %fusion.48 = f32[512,1024]{0,1:T(8,128)} fusion(f32[6,128,512]{2,1,0:T(8,128)} %param.19, f32[6,128,512]{2,1,0:T(8,128)} %copy.163, f32[6,128,512]{2,1,0:T(8,128)} %copy.162), kind=kOutput, calls=%fused_computation.79 | convolution fusion | flops 4832624640 | bytes 6815744 | tf_op jit(solution)/shard_map/bld,ble->de/dot_general | solution.py:96
  409.7 8.1 %convolution_bitcast_fusion.4 = f32[512,512]{1,0:T(8,128)} fusion(f32[3,256,512]{2,1,0:T(8,128)} %copy-done.12, f32[3,256,512]{1,2,0:T(8,128)} %bitcast.173), kind=kOutput, calls=%fused_computation.106 | convolution fusion | flops 2415919104 | bytes 4194304 | tf_op jit(solution)/shard_map/bld,ble->de/dot_general | solution.py:96
  417.8 5.4 convolution_add_fusion
  423.3 3.7 convolution_bitcast_fusion.5
  426.9 2.9 multiply_reduce_fusion.7
  429.9 8.0 fusion.10
  437.9 6.7 multiply_multiply_fusion
  444.5 7.6 fusion.101
  452.1 5.1 fusion.100
  457.3 3.0 copy.157
  460.3 3.0 copy.158
  463.3 3.0 copy.159
  466.4 10.8 %multiply_reduce_fusion.4 = (f32[512]{0:T(512)S(1)}, f32[3,256]{1,0:T(4,128)S(1)}, f32[3,256]{1,0:T(4,128)S(1)}, f32[512]{0:T(512)S(1)}, f32[3,256,512]{2,1,0:T(8,128)S(1)}) fusion(f32[3,256]{1,0:T(4,128)S(1)} %add_rsqrt_fusion.1, f32[3,256]{1,0:T(4,128)S(1)} %broadcast_multiply_fusion.6, f32[3,512]{1,0:T(4,128)S(1)} %fusion.82, f32[512]{0:T(512)S(1)} %copy-done.51, ...), kind=kOutput, calls=%fused_computation.82 | convolution fusion | flops 7255225856 | bytes 11042816 | tf_op jit(solution)/shard_map/dot_general | solution.py:189
  477.2 10.0 %fusion.26 = f32[512,1536]{1,0:T(8,128)} fusion(f32[3,256,512]{2,1,0:T(8,128)S(1)} %copy-done.46, f32[3,256,512]{2,1,0:T(8,128)S(1)} %copy-done.45, f32[3,256,512]{2,1,0:T(8,128)S(1)} %copy-done.44, f32[512]{0:T(512)S(1)} %copy-done.56, f32[512]{0:T(512)S(1)} %copy-done.53, f32[3,256]{1,0:T(4,128)S(1)} %add_rsqrt_fusion.1, ...), kind=kOutput, calls=%fused_computation.52 | convolution fusion | flops 7253262336 | bytes 9461760 | tf_op jit(solution)/shard_map/bld,ble->de/dot_general | solution.py:96
  487.2 2.0 multiply_reduce_fusion.5
  490.2 16.8 %fusion.52 = f32[3,256,512]{2,1,0:T(8,128)} fusion(f32[3,256,512]{2,1,0:T(8,128)} %copy-done.6, f32[2048,512]{1,0:T(8,128)} %param.34, f32[3,256,2048]{2,1,0:T(8,128)} %copy-done.4, f32[3,256,2048]{2,1,0:T(8,128)} %copy-done.3), kind=kOutput, calls=%fused_computation.102 | convolution fusion | flops 9667215360 | bytes 19922944 | tf_op jit(solution)/shard_map/dot_general | solution.py:158
  507.0 6.2 fusion.43
  513.2 40.8 %all-reduce = (f32[512]{0:T(512)}, f32[512]{0:T(512)}, f32[512]{0:T(512)}, f32[512]{0:T(512)}, f32[512]{0:T(512)}) all-reduce(f32[512]{0:T(512)S(1)} %get-tuple-element.115, f32[512]{0:T(512)S(1)} %get-tuple-element.107, f32[512]{0:T(512)S(1)} %get-tuple-element.114, ...), channel_id=1, replica_groups=mesh['dp'=16,'src'=2] {'dp','src'}, use_global_device_ids=true, to_apply=%region_18.0 | all-reduce | flops 2560 | bytes 20480 | tf_op jit(solution)/shard_map/psum | solution.py:211
  554.0 2.8 broadcast_multiply_fusion
  556.8 221.4 %all-reduce.4.cloned.1.call-done = (f32[50,512]{1,0:T(8,128)}, f32[512,1536]{1,0:T(8,128)}, f32[512,512]{1,0:T(8,128)}, f32[512,512]{1,0:T(8,128)}, f32[512,1024...) async-done(((f32[50,512]{1,0:T(8,128)}, f32[512,1536]{1,0:T(8,128)}, f32[512,512]{1,0:T(8,128)}, f32[512,512]{1,0:T(8,128)}, ...) | async-done | bytes 16879632 | tf_op jit(solution)/shard_map/psum | solution.py:211
  778.3 2.9 copy.170
  781.8 3.9 copy.202
  788.8 2.1 copy.206
  792.5 2.0 copy.207
  (166 shorter events, 18.9 us)
Async XLA Ops:
  7.2 6.4 copy-start
  7.2 6.4 copy-start.51
  7.2 6.4 copy-start.53
  7.2 6.4 copy-start.56
  7.2 96.3 %all-gather.7.cloned.1.call-start = ((), (), s32[]{:S(2)}) async-start(), calls=%async_computation.1 | async-start | bytes 4718592 | tf_op jit(solution)/shard_map/all_gather | solution.py:142
  7.3 5.0 copy-start.9
  43.4 4.8 copy-start.10
  43.4 4.8 copy-start.42
  48.2 3.1 copy-start.22
  48.3 3.1 copy-start.40
  51.4 4.3 copy-start.12
  55.7 145.8 %all-gather.11.cloned.1.call-start = ((), (), s32[]{:S(2)}) async-start(), calls=%async_computation.4 | async-start | bytes 9437184 | tf_op jit(solution)/shard_map/all_gather | solution.py:14
  103.5 10.7 %copy-start.20 = (f32[6,128,512]{1,2,0:T(8,128)S(1)}, f32[6,128,512]{1,2,0:T(8,128)}, u32[]{:S(2)}) copy-start(f32[6,128,512]{1,2,0:T(8,128)} %copy.143) | copy-start | bytes 4718596
  120.4 198.5 %all-gather.9.cloned.1.call-start = ((), (), s32[]{:S(2)}) async-start(), calls=%async_computation.2 | async-start | bytes 4718592 | tf_op jit(solution)/shard_map/all_gather | solution.py:169
  205.5 4.9 copy-start.24
  207.6 3.2 copy-start.36
  207.6 3.2 copy-start.52
  207.6 3.2 copy-start.55
  210.5 58.8 %copy-start.6 = (f32[3,256,512]{2,1,0:T(8,128)}, f32[3,256,512]{2,1,0:T(8,128)S(1)}, u32[]{:S(2)}) copy-start(f32[3,256,512]{2,1,0:T(8,128)S(1)} %get-tuple-element.145) | copy-start | bytes 4718596
  224.4 13.8 %copy-start.3 = (f32[3,256,2048]{2,1,0:T(8,128)}, f32[3,256,2048]{2,1,0:T(8,128)S(1)}, u32[]{:S(2)}) copy-start(f32[3,256,2048]{2,1,0:T(8,128)S(1)} %get-tuple-element.146) | copy-start | bytes 18874372
  224.4 13.8 %copy-start.31 = (f32[3,256,512]{2,1,0:T(8,128)S(1)}, f32[3,256,512]{2,1,0:T(8,128)}, u32[]{:S(2)}) copy-start(f32[3,256,512]{2,1,0:T(8,128)} %param.35) | copy-start | bytes 4718596
  238.2 15.7 %copy-start.4 = (f32[3,256,2048]{2,1,0:T(8,128)}, f32[3,256,2048]{2,1,0:T(8,128)S(1)}, u32[]{:S(2)}) copy-start(f32[3,256,2048]{2,1,0:T(8,128)S(1)} %fusion) | copy-start | bytes 18874372
  253.9 15.4 %copy-start.30 = (f32[3,256,2048]{2,1,0:T(8,128)}, f32[3,256,2048]{2,1,0:T(8,128)S(1)}, u32[]{:S(2)}) copy-start(f32[3,256,2048]{2,1,0:T(8,128)S(1)} %multiply_add_fusion) | copy-start | bytes 18874372
  269.9 3.9 copy-start.14
  273.8 135.9 %reduce-scatter.2.cloned.1.call-start = ((), (), s32[]{:S(2)}) async-start(), calls=%async_computation.3 | async-start | bytes 4718592 | tf_op jit(solution)/shard_map/reduce_scatter | solution.py:173
  318.9 5.6 copy-start.8
  318.9 5.6 copy-start.21
  324.5 11.9 %copy-start.25 = (f32[6,128,512]{1,2,0:T(8,128)S(1)}, f32[6,128,512]{1,2,0:T(8,128)}, u32[]{:S(2)}) copy-start(f32[6,128,512]{1,2,0:T(8,128)} %copy.145) | copy-start | bytes 4718596
  333.6 2.7 copy-start.5
  341.8 436.5 %all-reduce.4.cloned.1.call-start = ((), (), s32[]{:S(2)}) async-start(), calls=%async_computation.5 | async-start | bytes 33783808 | tf_op jit(solution)/shard_map/psum | solution.py:211
  341.8 5.7 copy-start.7
  341.9 20.6 %slice-start.2 = ((s8[6291456]{0:T(1024)(128)(4,1)}), s8[4194304]{0:T(1024)(128)(4,1)S(1)}, s32[]{:S(2)}) async-start(s8[6291456]{0:T(1024)(128)(4,1)} %bitcast.147), calls=%async_computation.8 | async-start | bytes 8388608
  341.9 20.6 %slice-start.4 = ((s8[6291456]{0:T(1024)(128)(4,1)}), s8[4194304]{0:T(1024)(128)(4,1)S(1)}, s32[]{:S(2)}) async-start(s8[6291456]{0:T(1024)(128)(4,1)} %bitcast.149), calls=%async_computation.10 | async-start | bytes 8388608
  347.6 14.9 %slice-start.3 = ((s8[6291456]{0:T(1024)(128)(4,1)}), s8[2097152]{0:T(1024)(128)(4,1)S(1)}, s32[]{:S(2)}) async-start(s8[6291456]{0:T(1024)(128)(4,1)} %bitcast.147), calls=%async_computation.9 | async-start | bytes 4194304
  347.6 14.9 %slice-start.5 = ((s8[6291456]{0:T(1024)(128)(4,1)}), s8[2097152]{0:T(1024)(128)(4,1)S(1)}, s32[]{:S(2)}) async-start(s8[6291456]{0:T(1024)(128)(4,1)} %bitcast.149), calls=%async_computation.11 | async-start | bytes 4194304
  347.6 14.9 %copy-start.32 = (f32[3,256,512]{2,1,0:T(8,128)S(1)}, f32[3,256,512]{2,1,0:T(8,128)}, u32[]{:S(2)}) copy-start(f32[3,256,512]{2,1,0:T(8,128)} %param.35) | copy-start | bytes 4718596
  347.6 27.0 %slice-start.6 = ((s8[6291456]{0:T(1024)(128)(4,1)}), s8[4194304]{0:T(1024)(128)(4,1)S(1)}, s32[]{:S(2)}) async-start(s8[6291456]{0:T(1024)(128)(4,1)} %bitcast.151), calls=%async_computation.12 | async-start | bytes 8388608
  362.5 12.1 %slice-start.7 = ((s8[6291456]{0:T(1024)(128)(4,1)}), s8[2097152]{0:T(1024)(128)(4,1)S(1)}, s32[]{:S(2)}) async-start(s8[6291456]{0:T(1024)(128)(4,1)} %bitcast.151), calls=%async_computation.13 | async-start | bytes 4194304
  362.5 12.1 %copy-start.28 = (f32[6,256,8,64]{1,3,2,0:T(8,128)S(1)}, f32[6,256,8,64]{1,3,2,0:T(8,128)}, u32[]{:S(2)}) copy-start(f32[6,256,8,64]{1,3,2,0:T(8,128)} %all-gather.7.cloned.1.call-done) | copy-start | bytes 9437188
  409.7 8.1 %copy-start.15 = (f32[3,256,512]{2,1,0:T(8,128)S(1)}, f32[3,256,512]{2,1,0:T(8,128)}, u32[]{:S(2)}) copy-start(f32[3,256,512]{2,1,0:T(8,128)} %copy-done.14) | copy-start | bytes 4718596
  409.7 8.1 %copy-start.35 = (f32[3,256,8,64]{1,3,2,0:T(8,128)S(1)}, f32[3,256,8,64]{1,3,2,0:T(8,128)}, u32[]{:S(2)}) copy-start(f32[3,256,8,64]{1,3,2,0:T(8,128)} %reduce-scatter.2.cloned.1.call-done) | copy-start | bytes 4718596
  409.7 8.1 %copy-start.41 = (f32[512,512]{1,0:T(8,128)S(1)}, f32[512,512]{1,0:T(8,128)}, u32[]{:S(2)}) copy-start(f32[512,512]{1,0:T(8,128)} %param.28) | copy-start | bytes 3145732
  417.8 5.4 copy-start.23
  417.8 12.0 %slice-start = ((s8[6291456]{0:T(1024)(128)(4,1)}), s8[4194304]{0:T(1024)(128)(4,1)S(1)}, s32[]{:S(2)}) async-start(s8[6291456]{0:T(1024)(128)(4,1)} %bitcast.145), calls=%async_computation.6 | async-start | bytes 8388608
  423.2 3.7 copy-start.16
  423.3 3.7 copy-start.43
  423.3 6.6 slice-start.1
  429.8 8.0 %copy-start.34 = (f32[3,256,512]{1,2,0:T(8,128)S(1)}, f32[3,256,512]{1,2,0:T(8,128)}, u32[]{:S(2)}) copy-start(f32[3,256,512]{1,2,0:T(8,128)} %copy.138) | copy-start | bytes 4718596
  437.9 6.7 copy-start.19
  444.5 7.6 copy-start.18
  466.3 10.8 %copy-start.11 = (f32[3,256,512]{2,1,0:T(8,128)S(1)}, f32[3,256,512]{2,1,0:T(8,128)}, u32[]{:S(2)}) copy-start(f32[3,256,512]{2,1,0:T(8,128)} %param.18) | copy-start | bytes 4718596
  466.3 10.8 %copy-start.44 = (f32[3,256,512]{2,1,0:T(8,128)S(1)}, f32[3,256,512]{2,1,0:T(8,128)}, u32[]{:S(2)}) copy-start(f32[3,256,512]{2,1,0:T(8,128)} %copy.157) | copy-start | bytes 4718596
  466.3 10.8 %copy-start.45 = (f32[3,256,512]{2,1,0:T(8,128)S(1)}, f32[3,256,512]{2,1,0:T(8,128)}, u32[]{:S(2)}) copy-start(f32[3,256,512]{2,1,0:T(8,128)} %copy.158) | copy-start | bytes 4718596
  466.3 10.8 %copy-start.46 = (f32[3,256,512]{2,1,0:T(8,128)S(1)}, f32[3,256,512]{2,1,0:T(8,128)}, u32[]{:S(2)}) copy-start(f32[3,256,512]{2,1,0:T(8,128)} %copy.159) | copy-start | bytes 4718596
  477.2 10.0 %copy-start.17 = (f32[3,256,512]{2,1,0:T(8,128)S(1)}, f32[3,256,512]{2,1,0:T(8,128)}, u32[]{:S(2)}) copy-start(f32[3,256,512]{2,1,0:T(8,128)} %copy-done.16) | copy-start | bytes 4718596
  490.1 16.8 %copy-start.26 = (f32[6,128,512]{2,1,0:T(8,128)S(1)}, f32[6,128,512]{2,1,0:T(8,128)}, u32[]{:S(2)}) copy-start(f32[6,128,512]{2,1,0:T(8,128)} %copy.162) | copy-start | bytes 4718596
  490.2 16.8 %copy-start.27 = (f32[6,128,512]{2,1,0:T(8,128)S(1)}, f32[6,128,512]{2,1,0:T(8,128)}, u32[]{:S(2)}) copy-start(f32[6,128,512]{2,1,0:T(8,128)} %copy.163) | copy-start | bytes 4718596
  490.2 16.8 %copy-start.29 = (f32[512,1024]{1,0:T(8,128)S(1)}, f32[512,1024]{1,0:T(8,128)}, u32[]{:S(2)}) copy-start(f32[512,1024]{1,0:T(8,128)} %param.29) | copy-start | bytes 6291460
  778.3 2.9 copy-start.50
  781.8 3.9 copy-start.49
  781.8 4.9 copy-start.48
  781.8 5.9 copy-start.47
  785.7 3.1 copy-start.38
  788.8 3.7 copy-start.37
  (6 other events, 14.2 us)
Sparse Core Ops, SparseCore 0:
  55.8 47.6 all-gather.6
  120.5 80.8 all-gather.10
  273.9 44.9 all-gather.8
  341.9 43.3 reduce-scatter.1
  490.3 287.9 all-reduce.3
where the time goes:
time: 811 us; the launch traced here: 802 us
  waiting for transfers between devices  365 us (45%)
  matrix products  270 us (33%)
  local copies, waits for them, and re-layouts  60.6 us (7%)
  blocking collectives  51.3 us (6%)
  other arithmetic  39.1 us (5%)
  between operations  15.1 us (2%)
    psum x1, waiting for transfers between devices, shards(): lax.psum((time_g, mask_g, first_gain_g, first_bias_g, self_qkv_g, self_ou...  221 us
    all_gather x1, waiting for transfers between devices, combined_all(): everything = jax.tree.map(lambda part: lax.all_gather(part, axis), x)  66.4 us
    dot_general x7, matrix products, weight_grad(): return jnp.einsum('bld,ble->de', left, right, precision=precise)  63.3 us
    all_gather x1, waiting for transfers between devices, shards(): group_grads = lax.all_gather(grad_cross, 'src', axis=0, tiled=True)  45 us
    psum x1, blocking collectives, shards(): lax.psum((time_g, mask_g, first_gain_g, first_bias_g, self_qkv_g, self_ou...  40.8 us
    all_gather x1, waiting for transfers between devices, shards(): group_queries = lax.all_gather(query_heads, 'src', axis=0, tiled=True)  31.9 us
    unnamed x138, local copies, waits for them, and re-layouts  25.5 us
    dot_general x2, matrix products, attend_grads(): jnp.einsum('bhqk,bqhe->bkhe', weights, grad_out, precision=precise)  20.3 us
  transfers between devices with their start and end apart: 5, of which 4 were waited for; matrix products, arithmetic and copies ran while one was open for 14% of the time, Pallas kernels for 0%

commit v1 on v0

v1 whole, which is shorter than its diff:
```python
import functools

import jax
import jax.numpy as jnp
from jax import lax
from jax.experimental import pallas as pl
from jax.experimental.pallas import tpu as pltpu
from jax.sharding import PartitionSpec as P

HEADS = 8
EPSILON = 1e-05
ALL = ("dp", "src")
f32 = jnp.float32
bf16 = jnp.bfloat16
VMEM_LIMIT = 56 * 2**20


def split(values):
    high = values.astype(bf16)
    return high, (values - high.astype(f32)).astype(bf16)


def dot(left, right, left_dim, right_dim):
    return lax.dot_general(
        left, right, (((left_dim,), (right_dim,)), ((), ())), preferred_element_type=f32
    )


def three(left, right, left_dim=1, right_dim=0):
    left_high, left_low = left
    right_high, right_low = right
    return (
        dot(left_high, right_high, left_dim, right_dim)
        + dot(left_high, right_low, left_dim, right_dim)
        + dot(left_low, right_high, left_dim, right_dim)
    )


def keep_split(ref, values):
    high, low = split(values)
    ref[0] = high
    ref[1] = low


def pair_of(ref):
    return ref[0], ref[1]


def norm(values):
    centred = values - jnp.mean(values, -1, keepdims=True)
    inverse = lax.rsqrt(jnp.mean(centred * centred, -1, keepdims=True) + EPSILON)
    return centred * inverse, inverse


def norm_back(grad_out, normed, inverse, gain):
    scaled = grad_out * gain
    return inverse * (
        scaled
        - jnp.mean(scaled, -1, keepdims=True)
        - normed * jnp.mean(scaled * normed, -1, keepdims=True)
    )


def half_masks(shape):
    lane = lax.broadcasted_iota(jnp.int32, shape, 1)
    size = shape[1] // 2
    return [lane < size, lane >= size]


def scores(masked, other):
    high, low = masked
    other_high, other_low = other
    return dot(
        jnp.concatenate([high, low], 1), jnp.concatenate([other_high, other_high], 1), 1, 1
    ) + dot(high, other_low, 1, 1)


def spread(weights, values, dim):
    high, low = weights
    value_high, value_low = values
    both = dot(high, jnp.concatenate([value_high, value_low], 1), dim, 0)
    size = value_high.shape[1]
    return both[:, :size] + both[:, size:] + dot(low, value_high, dim, 0)


def attend(queries, keys, values, weights_ref, out_ref):
    size = 2 * queries.shape[1] // HEADS
    masks = half_masks((queries.shape[0], size))
    key_masks = half_masks((keys.shape[0], size))
    scale = (size // 2) ** (-0.5)
    for pair in range(HEADS // 2):
        lanes = slice(pair * size, (pair + 1) * size)
        pair_queries = queries[:, lanes] * scale
        pair_keys = split(keys[:, lanes])
        pair_values = values[:, lanes]
        total = 0.0
        for e in range(2):
            score = scores(split(jnp.where(masks[e], pair_queries, 0.0)), pair_keys)
            exponent = jnp.exp(score - jnp.max(score, -1, keepdims=True))
            weights = exponent * (1.0 / jnp.sum(exponent, -1, keepdims=True))
            weights_ref[0, 2 * pair + e] = weights
            total = total + spread(
                split(weights), split(jnp.where(key_masks[e], pair_values, 0.0)), 1
            )
        out_ref[:, lanes] = total


def attend_back(queries, keys, values, weights_ref, grad, attended, put):
    size = 2 * queries.shape[1] // HEADS
    masks = half_masks((queries.shape[0], size))
    key_masks = half_masks((keys.shape[0], size))
    scale = (size // 2) ** (-0.5)
    for pair in range(HEADS // 2):
        lanes = slice(pair * size, (pair + 1) * size)
        pair_queries = queries[:, lanes] * scale
        pair_keys = keys[:, lanes]
        pair_values = split(values[:, lanes])
        pair_grad = grad[:, lanes]
        pair_dots = pair_grad * attended[:, lanes]
        grad_queries = grad_keys = grad_values = 0.0
        for e in range(2):
            head_grad = split(jnp.where(masks[e], pair_grad, 0.0))
            dots = jnp.sum(jnp.where(masks[e], pair_dots, 0.0), -1, keepdims=True)
            weights = weights_ref[0, 2 * pair + e]
            grad_scores = split(weights * (scores(head_grad, pair_values) - dots))
            grad_queries = grad_queries + spread(
                grad_scores, split(jnp.where(key_masks[e], pair_keys, 0.0)), 1
            )
            grad_keys = grad_keys + spread(
                grad_scores, split(jnp.where(masks[e], pair_queries, 0.0)), 0
            )
            grad_values = grad_values + spread(split(weights), head_grad, 0)
        put(lanes, grad_queries * scale, grad_keys, grad_values)


def self_forward(
    stamps,
    inputs,
    chosen,
    time_table,
    mask_vector,
    gain,
    bias,
    qkv_weight,
    out_weight,
    query_weight,
    normed_out,
    inverse_out,
    qkv_out,
    weights_out,
    attended_out,
    middle_out,
    query_out,
    qkv_split,
    out_split,
    query_split,
):
    item = pl.program_id(0)

    @pl.when(item == 0)
    def _():
        keep_split(qkv_split, qkv_weight[...])
        keep_split(out_split, out_weight[...])
        keep_split(query_split, query_weight[...])

    flags = chosen[0]
    start = (
        inputs[0] * (1.0 - flags)
        + flags * mask_vector[...]
        + time_table[pl.ds(stamps[item], 1), :]
    )
    normed, inverse = norm(start)
    normed_out[0] = normed
    inverse_out[0] = inverse
    packed = three(split(normed * gain[...] + bias[...]), pair_of(qkv_split))
    qkv_out[0] = packed
    width = start.shape[1]
    attend(
        packed[:, :width],
        packed[:, width : 2 * width],
        packed[:, 2 * width :],
        weights_out,
        attended_out.at[0],
    )
    middle = start + three(split(attended_out[0]), pair_of(out_split))
    middle_out[0] = middle
    query_out[0] = three(split(middle), pair_of(query_split))


def cross_forward(
    place,
    memory_own,
    memory_far,
    queries,
    middle,
    kv_weight,
    out_weight,
    kv_out,
    weights_out,
    attended_out,
    after_out,
    kv_split,
    out_split,
):
    @pl.when(pl.program_id(0) == 0)
    def _():
        keep_split(kv_split, kv_weight[...])
        keep_split(out_split, out_weight[...])

    memory = jnp.concatenate([memory_own[0], memory_far[0]], 0)
    pairs = three(split(memory), pair_of(kv_split))
    kv_out[0] = pairs
    width = memory.shape[1]
    attend(queries[0], pairs[:, :width], pairs[:, width:], weights_out, attended_out.at[0])
    after_out[0] = middle[0] + three(split(attended_out[0]), pair_of(out_split))


def feed(
    first,
    last,
    after,
    cotangent,
    gain,
    bias,
    expand,
    reduce,
    total_in,
    grad_in,
    total_out,
    grad_out,
    weight_grads,
    gain_grad,
    bias_grad,
    normed_split,
    cot_split,
    total,
    grad_normed,
):
    step = pl.program_id(0)

    @pl.when(step == 0)
    def _():
        normed, _ = norm(after[...])
        keep_split(normed_split, normed * gain[...] + bias[...])
        keep_split(cot_split, cotangent[...])
        if first:
            total[...] = after[...]
            grad_normed[...] = jnp.zeros_like(grad_normed)
        else:
            total[...] = total_in[...]
            grad_normed[...] = grad_in[...]

    width = after.shape[1]
    size = 256
    for k in range(expand.shape[1] // size):
        cols = slice(k * size, (k + 1) * size)
        expand_pair = split(expand[:, cols])
        reduce_pair = split(reduce[cols, :])
        pre = three(pair_of(normed_split), expand_pair)
        cdf = 0.5 * (1.0 + lax.erf(pre * (0.5**0.5)))
        slope = cdf + pre * (jnp.exp(-0.5 * pre * pre) * 0.3989422804014327)
        hidden = split(pre * cdf)
        total[...] += three(hidden, reduce_pair)
        weight_grads[0, 0, cols, :] = three(hidden, pair_of(cot_split), 0, 0)
        grad_pre = split(three(pair_of(cot_split), reduce_pair, 1, 1) * slope)
        weight_grads[0, 1, :, cols] = three(pair_of(normed_split), grad_pre, 0, 0)
        grad_normed[...] += three(grad_pre, expand_pair, 1, 1)

    @pl.when(step == pl.num_programs(0) - 1)
    def _():
        total_out[...] = total[...]
        if last:
            normed, inverse = norm(after[...])
            grad = grad_normed[...]
            gain_grad[...] = jnp.sum(grad * normed, 0, keepdims=True)
            bias_grad[...] = jnp.sum(grad, 0, keepdims=True)
            grad_out[...] = cotangent[...] + norm_back(grad, normed, inverse, gain[...])
        else:
            grad_out[...] = grad_normed[...]


def cross_backward(
    place,
    memory_own,
    memory_far,
    queries,
    middle,
    pairs,
    weights,
    attended,
    grad_after,
    out_weight,
    query_weight,
    kv_weight,
    own_grad,
    far_grad,
    middle_grad,
    weight_grads,
    out_split,
    query_split,
    kv_split,
    grad_queries,
    grad_pairs,
):
    item = pl.program_id(0)

    @pl.when(item == 0)
    def _():
        keep_split(out_split, out_weight[...])
        keep_split(query_split, query_weight[...])
        keep_split(kv_split, kv_weight[...])
        weight_grads[...] = jnp.zeros_like(weight_grads)

    width = middle.shape[2]
    upstream = grad_after[0]
    upstream_pair = split(upstream)
    grad = three(upstream_pair, pair_of(out_split), 1, 1)
    weight_grads[0] += three(split(attended[0]), upstream_pair, 0, 0)

    def put(lanes, query_part, key_part, value_part):
        grad_queries[:, lanes] = query_part
        grad_pairs[:, lanes] = key_part
        grad_pairs[:, lanes.start + width : lanes.stop + width] = value_part

    attend_back(
        queries[0],
        pairs[0, :, :width],
        pairs[0, :, width:],
        weights,
        grad,
        attended[0],
        put,
    )
    query_pair = split(grad_queries[...])
    middle_grad[0] = upstream + three(query_pair, pair_of(query_split), 1, 1)
    weight_grads[1] += three(split(middle[0]), query_pair, 0, 0)
    both = split(grad_pairs[...])
    memory_grad = three(both, pair_of(kv_split), 1, 1)
    half = own_grad.shape[1]
    own_grad[0] = memory_grad[:half]
    far_grad[0] = memory_grad[half:]
    memory_pair = split(jnp.concatenate([memory_own[0], memory_far[0]], 0))
    for k in range(2):
        cols = slice(k * width, (k + 1) * width)
        weight_grads[2 + k] += three(memory_pair, (both[0][:, cols], both[1][:, cols]), 0, 0)


def self_backward(
    stamps,
    normed,
    inverse,
    chosen,
    packed,
    weights,
    attended,
    grad_middle,
    gain,
    bias,
    qkv_weight,
    out_weight,
    input_grad,
    weight_grads,
    time_grad,
    mask_grad,
    gain_grad,
    bias_grad,
    qkv_split,
    out_split,
    grad_packed,
):
    item = pl.program_id(0)

    @pl.when(item == 0)
    def _():
        keep_split(out_split, out_weight[...])
        keep_split(qkv_split, qkv_weight[...])
        for ref in (weight_grads, time_grad, mask_grad, gain_grad, bias_grad):
            ref[...] = jnp.zeros_like(ref)

    width = normed.shape[2]
    upstream = grad_middle[0]
    upstream_pair = split(upstream)
    grad = three(upstream_pair, pair_of(out_split), 1, 1)
    weight_grads[0] += three(split(attended[0]), upstream_pair, 0, 0)

    def put(lanes, query_part, key_part, value_part):
        for k, part in enumerate((query_part, key_part, value_part)):
            grad_packed[:, lanes.start + k * width : lanes.stop + k * width] = part

    attend_back(
        packed[0, :, :width],
        packed[0, :, width : 2 * width],
        packed[0, :, 2 * width :],
        weights,
        grad,
        attended[0],
        put,
    )
    all_three = split(grad_packed[...])
    grad_normed = three(all_three, pair_of(qkv_split), 1, 1)
    unit = normed[0]
    normed_pair = split(unit * gain[...] + bias[...])
    for k in range(3):
        cols = slice(k * width, (k + 1) * width)
        weight_grads[1 + k] += three(
            normed_pair, (all_three[0][:, cols], all_three[1][:, cols]), 0, 0
        )
    gain_grad[...] += jnp.sum(grad_normed * unit, 0, keepdims=True)
    bias_grad[...] += jnp.sum(grad_normed, 0, keepdims=True)
    grad_start = upstream + norm_back(grad_normed, unit, inverse[0], gain[...])
    flags = chosen[0]
    input_grad[0] = grad_start * (1.0 - flags)
    mask_grad[...] += jnp.sum(grad_start * flags, 0, keepdims=True)
    row = pl.ds(stamps[item], 1)
    time_grad[row, :] += jnp.sum(grad_start, 0, keepdims=True)


def whole_spec(shape):
    return pl.BlockSpec(shape, lambda i, *_: (0,) * len(shape))


def item_spec(shape):
    return pl.BlockSpec((1,) + shape[1:], lambda i, *_: (i,) + (0,) * (len(shape) - 1))


def own_spec(shape, items):
    return pl.BlockSpec((1,) + shape[1:], lambda i, place: (place[0] * items + i, 0, 0))


def struct(*shape):
    return jax.ShapeDtypeStruct(shape, f32)


def call(kernel, grid, prefetch, ins, outs, scratch, flops, name):
    return pl.pallas_call(
        kernel,
        grid_spec=pltpu.PrefetchScalarGridSpec(
            num_scalar_prefetch=len(prefetch),
            grid=(grid,),
            in_specs=[spec for _, spec in ins],
            out_specs=[spec for _, spec in outs],
            scratch_shapes=scratch,
        ),
        out_shape=[out for out, _ in outs],
        compiler_params=pltpu.CompilerParams(
            dimension_semantics=("arbitrary",), vmem_limit_bytes=VMEM_LIMIT
        ),
        cost_estimate=pl.CostEstimate(flops=flops, bytes_accessed=0, transcendentals=0),
        name=name,
    )(*prefetch, *[array for array, _ in ins])


def split_scratch(*shape):
    return pltpu.VMEM((2,) + shape, bf16)


def whole(array):
    return (array, whole_spec(array.shape))


def by_item(array):
    return (array, item_spec(array.shape))


def shards(
    inputs,
    memory,
    timesteps,
    mask_flags,
    time_table,
    mask_vector,
    first_gain,
    first_bias,
    self_qkv,
    self_out,
    cross_query,
    cross_kv,
    cross_out,
    second_gain,
    second_bias,
    expand_weight,
    reduce_weight,
    cotangent,
):
    items, length, width = inputs.shape
    half = memory.shape[1]
    positions = 2 * half
    feed_width = expand_weight.shape[1]
    mac = items * length * width * width
    swap = [(0, 1), (1, 0)]
    src = lax.axis_index("src")
    place = src.astype(jnp.int32).reshape(1)

    memory_far = lax.ppermute(
        lax.dynamic_slice_in_dim(memory, (1 - src) * items, items, 0), "src", swap
    )
    chosen = mask_flags.astype(f32)[..., None]
    vectors = [v[None, :] for v in (mask_vector, first_gain, first_bias, second_gain, second_bias)]
    mask_row, first_gain_row, first_bias_row, second_gain_row, second_bias_row = vectors

    def rows_out(*shape):
        return (struct(*shape), item_spec(shape))

    def whole_out(*shape):
        return (struct(*shape), whole_spec(shape))

    normed, inverse, packed, self_weights, self_attended, middle, queries = call(
        self_forward,
        items,
        [timesteps],
        [
            by_item(inputs),
            by_item(chosen),
            whole(time_table),
            whole(mask_row),
            whole(first_gain_row),
            whole(first_bias_row),
            whole(self_qkv),
            whole(self_out),
            whole(cross_query),
        ],
        [
            rows_out(items, length, width),
            rows_out(items, length, 1),
            rows_out(items, length, 3 * width),
            rows_out(items, HEADS, length, length),
            rows_out(items, length, width),
            rows_out(items, length, width),
            rows_out(items, length, width),
        ],
        [
            split_scratch(width, 3 * width),
            split_scratch(width, width),
            split_scratch(width, width),
        ],
        6 * 6 * mac,
        "self_forward",
    )
    pairs, cross_weights, cross_attended, after = call(
        cross_forward,
        items,
        [place],
        [
            (memory, own_spec(memory.shape, items)),
            by_item(memory_far),
            by_item(queries),
            by_item(middle),
            whole(cross_kv),
            whole(cross_out),
        ],
        [
            rows_out(items, positions, 2 * width),
            rows_out(items, HEADS, length, positions),
            rows_out(items, length, width),
            rows_out(items, length, width),
        ],
        [split_scratch(width, 2 * width), split_scratch(width, width)],
        6 * 4 * mac,
        "cross_forward",
    )

    tokens = items * length
    after_flat = after.reshape(tokens, width)
    cot_flat = cotangent.reshape(tokens, width)
    blocks = feed_width // width
    part = blocks // 2
    total = grad = jnp.zeros((8, 128), f32)
    feed_grads = []
    for k in range(2):
        total, grad, weight_grads, second_gain_g, second_bias_g = call(
            functools.partial(feed, k == 0, k == 1),
            part,
            [],
            [
                whole(after_flat),
                whole(cot_flat),
                whole(second_gain_row),
                whole(second_bias_row),
                (
                    expand_weight,
                    pl.BlockSpec((width, width), lambda j, k=k: (0, j + k * part)),
                ),
                (
                    reduce_weight,
                    pl.BlockSpec((width, width), lambda j, k=k: (j + k * part, 0)),
                ),
                whole(total),
                whole(grad),
            ],
            [
                whole_out(tokens, width),
                whole_out(tokens, width),
                (
                    struct(part, 2, width, width),
                    pl.BlockSpec((1, 2, width, width), lambda j: (j, 0, 0, 0)),
                ),
                whole_out(1, width),
                whole_out(1, width),
            ],
            [
                split_scratch(tokens, width),
                split_scratch(tokens, width),
                pltpu.VMEM((tokens, width), f32),
                pltpu.VMEM((tokens, width), f32),
            ],
            6 * 12 * mac,
            f"feed_{k}",
        )
        feed_grads.append(weight_grads)
    output = total.reshape(items, length, width)
    grad_after = grad.reshape(items, length, width)

    memory_grad, far_grad, grad_middle, cross_grads = call(
        cross_backward,
        items,
        [place],
        [
            (memory, own_spec(memory.shape, items)),
            by_item(memory_far),
            by_item(queries),
            by_item(middle),
            by_item(pairs),
            by_item(cross_weights),
            by_item(cross_attended),
            by_item(grad_after),
            whole(cross_out),
            whole(cross_query),
            whole(cross_kv),
        ],
        [
            (struct(*memory.shape), own_spec(memory.shape, items)),
            rows_out(items, half, width),
            rows_out(items, length, width),
            whole_out(4, width, width),
        ],
        [
            split_scratch(width, width),
            split_scratch(width, width),
            split_scratch(width, 2 * width),
            pltpu.VMEM((length, width), f32),
            pltpu.VMEM((positions, 2 * width), f32),
        ],
        6 * 10 * mac,
        "cross_backward",
    )
    far_grad = lax.ppermute(far_grad, "src", swap)
    memory_grad = lax.dynamic_update_slice_in_dim(memory_grad, far_grad, (1 - src) * items, 0)

    steps = time_table.shape[0]
    input_grad, self_grads, time_g, mask_g, first_gain_g, first_bias_g = call(
        self_backward,
        items,
        [timesteps],
        [
            by_item(normed),
            by_item(inverse),
            by_item(chosen),
            by_item(packed),
            by_item(self_weights),
            by_item(self_attended),
            by_item(grad_middle),
            whole(first_gain_row),
            whole(first_bias_row),
            whole(self_qkv),
            whole(self_out),
        ],
        [
            rows_out(items, length, width),
            whole_out(4, width, width),
            whole_out(steps, width),
            whole_out(1, width),
            whole_out(1, width),
            whole_out(1, width),
        ],
        [
            split_scratch(width, 3 * width),
            split_scratch(width, width),
            pltpu.VMEM((length, 3 * width), f32),
        ],
        6 * 10 * mac,
        "self_backward",
    )

    small = jnp.concatenate([mask_g, first_gain_g, first_bias_g, second_gain_g, second_bias_g, time_g])
    groups = [
        feed_grads[0].reshape(-1, width),
        feed_grads[1].reshape(-1, width),
        cross_grads.reshape(-1, width),
        self_grads.reshape(-1, width),
    ]
    first, second, third, fourth, small = lax.psum((*groups, small), ALL)
    fed = jnp.concatenate([first.reshape(part, 2, width, width), second.reshape(part, 2, width, width)])
    reduce_g = fed[:, 0].reshape(feed_width, width)
    expand_g = jnp.transpose(fed[:, 1], (1, 0, 2)).reshape(width, feed_width)
    third = third.reshape(4, width, width)
    fourth = fourth.reshape(4, width, width)
    cross_kv_g = jnp.concatenate([third[2], third[3]], 1)
    self_qkv_g = jnp.concatenate([fourth[1], fourth[2], fourth[3]], 1)
    return (
        output,
        input_grad,
        memory_grad,
        small[5:],
        small[0],
        small[1],
        small[2],
        self_qkv_g,
        fourth[0],
        third[1],
        cross_kv_g,
        third[0],
        small[3],
        small[4],
        expand_g,
        reduce_g,
    )


def solution(mesh):
    tokens = P(("dp", "src"), None, None)
    placed = (tokens, P("dp", "src", None), P(("dp", "src")), P(("dp", "src"), None))
    return jax.shard_map(
        shards,
        mesh=mesh,
        in_specs=placed + (P(),) * 13 + (tokens,),
        out_specs=(tokens, tokens, P("dp", "src", None)) + (P(),) * 13,
        check_vma=False,
    )
```

time: 811 us -> 494 us (0.61)
  matrix products: 270 us -> 0 us
  Pallas kernels: 0 us -> 143 us
  waiting for transfers between devices: 365 us -> 288 us
  blocking collectives: 51.3 us -> 0 us
  other arithmetic: 39.1 us -> 4.06 us
  local copies, waits for them, and re-layouts: 60.6 us -> 35.4 us
    dot_general x35 -> x0, matrix products: 270 us -> none  [the longest x7 63.3 us: weight_grad(): return jnp.einsum('bld,ble->de', left, right, precision=precise)]
    all_gather x3 -> x0, waiting for transfers between devices: 143 us -> none  [the longest x1 66.4 us: combined_all(): everything = jax.tree.map(lambda part: lax.all_gather(part, axis), x)]
    pallas_call x0 -> x6, Pallas kernels: none -> 143 us  [call(): pl.pallas_call(kernel, grid_spec=pltpu.PrefetchScalarGridSpec(num_scalar_...]
    psum x1 -> x0, blocking collectives: 40.8 us -> none  [shards(): lax.psum((time_g, mask_g, first_gain_g, first_bias_g, self_qkv_g, self_ou...]
    psum x1, waiting for transfers between devices: 221 us -> 255 us  [shards(): first, second, third, fourth, small = lax.psum((*groups, small), ALL)]
    ppermute x0 -> x2, waiting for transfers between devices: none -> 32.5 us  [the longest x1 32.5 us: shards(): far_grad = lax.ppermute(far_grad, 'src', swap)]
    reduce_sum x7 -> x0, other arithmetic: 16 us -> none  [the longest x1 5.55 us: attend_grads(): row_dots = jnp.sum(grad_out * attended, -1)]
    reshape x5 -> x0, local copies, waits for them, and re-layouts: 15.2 us -> none  [joined(): values.reshape(values.shape[0], values.shape[1], values.shape[2] * values...]
  transfers between devices with their start and end apart: 5 -> 3, of which waited for: 4 -> 2; matrix products, arithmetic and copies ran while one was open for 14% -> 0% of each run, Pallas kernels for 0% -> 4%
where the time goes in v1:
time: 494 us; the launch traced here: 487 us
  waiting for transfers between devices  288 us (58%)
  Pallas kernels  143 us (29%)
  local copies, waits for them, and re-layouts  35.4 us (7%)
  between operations  14.3 us (3%)
    psum x1, waiting for transfers between devices, shards(): first, second, third, fourth, small = lax.psum((*groups, small), ALL)  255 us
    pallas_call x6, Pallas kernels, call(): pl.pallas_call(kernel, grid_spec=pltpu.PrefetchScalarGridSpec(num_scalar_...  143 us
    ppermute x1, waiting for transfers between devices, shards(): far_grad = lax.ppermute(far_grad, 'src', swap)  32.5 us
    unnamed x16, local copies, waits for them, and re-layouts  10.8 us
  transfers between devices with their start and end apart: 3, of which 2 were waited for; matrix products, arithmetic and copies ran while one was open for 0% of the time, Pallas kernels for 4%

profile of v1, /device:TPU:0, one launch (start us, length us, event | category | flops | bytes accessed | tf_op | source)
XLA Modules:
  0.0 487.5 jit_solution(7034048275497604637)
XLA Ops:
  7.2 0.0 all-reduce.3.cloned.1.call-start
  7.2 1.2 constant_dynamic-slice_fusion
  8.4 3.0 collective-permute-start
  11.5 0.7 convert_bitcast_fusion
  12.1 0.9 copy.34.chosen
  13.1 19.3 %self_forward.1 = (f32[3,256,512]{2,1,0:T(8,128)}, f32[3,256,1]{2,1,0:T(8,128)}, f32[3,256,1536]{2,1,0:T(8,128)}, f32[3,8,256,256]{3,2,1,0:T(8,128)}, f32[3,256,...) custom-call(s32[3]{0:T(128)} %stamps.3, f32[3,256,512]{2,1,0:T(8,128)} %inputs.1, ...), custom_call_target="tpu_custom_call" | custom-call | flops 7247757312 | tf_op jit(solution)/shard_map/self_forward/pallas_call | solution.py:435
  32.4 0.0 collective-permute-done.memory_far
  32.4 0.0 copy-start.6
  32.4 0.9 copy-done.6
  33.3 14.3 %cross_forward.1 = (f32[3,256,1024]{2,1,0:T(8,128)}, f32[3,8,256,256]{3,2,1,0:T(8,128)}, f32[3,256,512]{2,1,0:T(8,128)}, f32[3,256,512]{2,1,0:T(8,128)}) custom-call(s32[1]{0:T(128)} %bitcast.place, f32[6,128,512]{2,1,0:T(8,128)} %memory_own.3, f32[3,128,512]{2,1,0:T(8,128)} %copy-done.6, f32[3,256,512]{2,1,0:T(8,128)} %get-tuple-element.45.queries, ...), custom_call_target="tpu_custom_call" | custom-call | flops 4831838208 | tf_op jit(solution)/shard_map/cross_forward/pallas_call | solution.py:435
  47.6 0.6 broadcast_in_dim.27.total_in.grad_in
  48.2 24.4 %feed_0.1 = (f32[768,512]{1,0:T(8,128)}, f32[768,512]{1,0:T(8,128)}, f32[2,2,512,512]{3,2,1,0:T(8,128)}, f32[1,512]{1,0:T(1,128)}, f32[1,512]{1,0:T(1,128)}) custom-call(f32[768,512]{1,0:T(8,128)} %bitcast.46, f32[768,512]{1,0:T(8,128)} %bitcast.34, f32[1,512]{1,0:T(1,128)} %bitcast.37, f32[1,512]{1,0:T(1,128)} %bitcast.39, f32[512,2048]{1,0:T(8,128)} %expand.3, ...), custom_call_target="tpu_custom_call" | custom-call | flops 14495514624 | tf_op jit(solution)/shard_map/feed_0/pallas_call | solution.py:435
  72.6 26.2 %feed_1.1 = (f32[768,512]{1,0:T(8,128)}, f32[768,512]{1,0:T(8,128)}, f32[2,2,512,512]{3,2,1,0:T(8,128)}, f32[1,512]{1,0:T(1,128)}, f32[1,512]{1,0:T(1,128)}) custom-call(f32[768,512]{1,0:T(8,128)} %bitcast.47, f32[768,512]{1,0:T(8,128)} %bitcast.35, f32[1,512]{1,0:T(1,128)} %bitcast.38, f32[1,512]{1,0:T(1,128)} %bitcast.40, f32[512,2048]{1,0:T(8,128)} %expand.3, ...), custom_call_target="tpu_custom_call" | custom-call | flops 14495514624 | tf_op jit(solution)/shard_map/feed_1/pallas_call | solution.py:435
  98.8 29.2 %cross_backward.1 = (f32[6,128,512]{2,1,0:T(8,128)}, f32[3,128,512]{2,1,0:T(8,128)}, f32[3,256,512]{2,1,0:T(8,128)}, f32[4,512,512]{2,1,0:T(8,128)}) custom-call(s32[1]{0:T(128)} %bitcast.place, f32[6,128,512]{2,1,0:T(8,128)} %memory_own.3, f32[3,128,512]{2,1,0:T(8,128)} %copy-done.6, f32[3,256,512]{2,1,0:T(8,128)} %get-tuple-element.45.queries, ...), custom_call_target="tpu_custom_call" | custom-call | flops 12079595520 | tf_op jit(solution)/shard_map/cross_backward/pallas_call | solution.py:435
  128.0 0.0 copy-start.1
  128.0 0.0 copy-start.2
  128.0 29.5 %self_backward.1 = (f32[3,256,512]{2,1,0:T(8,128)}, f32[4,512,512]{2,1,0:T(8,128)}, f32[50,512]{1,0:T(8,128)}, f32[1,512]{1,0:T(1,128)}, f32[1,512]{1,0:T(1,128)}, /*index=5*/f32[1,512]{1,0:T(1,128)}) custom-call(s32[3]{0:T(128)} %stamps.3, f32[3,256,512]{2,1,0:T(8,128)} %get-tuple-element.51.normed, f32[3,256,1]{2,1,0:T(8,128)} %get-tuple-element.52.inverse, ...), custom_call_target="tpu_custom_call" | custom-call | flops 12079595520 | tf_op jit(solution)/shard_map/self_backward/pallas_call | solution.py:435
  157.5 0.0 copy-done.1
  157.5 0.0 copy-done.2
  157.5 2.9 concatenate.12
  160.4 0.0 copy-start.5
  160.4 0.0 copy-start.3
  160.4 0.0 all-reduce.3.cloned.1.call-update
  160.4 1.1 copy-done.5
  161.5 0.0 collective-permute-start.1
  161.5 32.5 %collective-permute-done.1 = f32[3,128,512]{2,1,0:T(8,128)S(1)} collective-permute-done((f32[3,128,512]{2,1,0:T(8,128)S(1)}, f32[3,128,512]{2,1,0:T(8,128)S(1)}, u32[]{:S(2)}, u32[]{:S(2)}) %collective-permute-start.1) | collective-permute-done | bytes 786464 | tf_op jit(solution)/shard_map/ppermute | solution.py:646
  194.0 0.0 copy-done.3
  194.0 0.1 constant_dynamic-update-slice_fusion.2
  194.1 0.0 copy-start.4
  194.1 255.3 %all-reduce.3.cloned.1.call-done = (f32[55,512]{1,0:T(8,128)}, f32[2048,512]{1,0:T(8,128)}, f32[2048,512]{1,0:T(8,128)}, f32[2,2,512,512]{3,2,1,0:T(8,128)}, f32[2,2,512,512]{3,2,1,0:T(8,128)}) async-done(((f32[55,512]{1,0:T(8,128)}, f32[2048,512]{1,0:T(8,128)}, f32[2048,512]{1,0:T(8,128)}, f32[2,2,512,512]{3,2,1,0:T(8,128)}, f32[2,2,512,512]{3,2,1,0:T(8,128)}), (f32[55,512]{1,0:T(8,128)}, ...) | async-done | bytes 16889872 | tf_op jit(solution)/shard_map/psum | solution.py:691
  449.3 1.5 fusion.3
  450.8 1.6 slice.72
  452.4 0.0 copy-start
  452.4 2.8 constant_dynamic-update-slice_fusion.1
  455.2 0.0 copy-done.4
  455.3 0.6 copy-done
  455.8 0.4 constant_dynamic-update-slice_fusion
  456.3 4.5 fusion
  460.7 5.3 %copy.36 = f32[512,4,512]{0,2,1:T(8,128)} copy(f32[512,4,512]{2,0,1:T(8,128)} %get-tuple-element.96) | data formatting | bytes 8388608 | tf_op jit(solution)/shard_map/transpose | solution.py:694
  466.0 5.3 %copy.37 = f32[512,2048]{1,0:T(8,128)} copy(f32[512,2048]{0,1:T(8,128)} %bitcast.25) | data formatting | bytes 8388608
  471.4 5.7 %fusion.1 = (f32[512,512]{1,0:T(8,128)}, f32[512,512]{1,0:T(8,128)S(1)}, f32[512,512]{1,0:T(8,128)S(1)}, f32[512,512]{1,0:T(8,128)}, f32[512,512]{1,0:T(8,128)S(...) fusion(f32[2048,512]{1,0:T(8,128)} %get-tuple-element.92, f32[2048,512]{1,0:T(8,128)} %get-tuple-element.91), kind=kLoop, calls=%fused_computation.9 | loop fusion | bytes 16777216 | tf_op jit(solution)/shard_map/slice | solution.py:711
  477.1 1.5 pad_maximum_fusion.1
  478.6 1.9 pad_maximum_fusion
Async XLA Ops:
  7.2 442.2 %all-reduce.3.cloned.1.call-start = ((), (), s32[]{:S(2)}) async-start(), calls=%async_computation | async-start | bytes 33783808 | tf_op jit(solution)/shard_map/psum | solution.py:691
  8.4 24.0 %collective-permute-start = (f32[3,128,512]{2,1,0:T(8,128)S(1)}, f32[3,128,512]{2,1,0:T(8,128)S(1)}, u32[]{:S(2)}, u32[]{:S(2)}) collective-permute-start(f32[3,128,512]{2,1,0:T(8,128)S(1)} %constant_dynamic-slice_fusion), channel_id=1, source_target_pairs={{0,1},{1,0},{2,3},{3,2},{4,5},{5,4},{6,7},{7,6},{8,9},{9,8},{10,11... | collective-permute-start | bytes 2359304 | tf_op jit(solution)/shard_map/ppermute | solution.py:494
  32.4 0.9 copy-start.6
  128.0 29.5 %copy-start.1 = (f32[1,512]{1,0:T(1,128)S(1)}, f32[1,512]{1,0:T(1,128)}, u32[]{:S(2)}) copy-start(f32[1,512]{1,0:T(1,128)} %get-tuple-element.67) | copy-start | bytes 6148
  128.0 29.5 %copy-start.2 = (f32[1,512]{1,0:T(1,128)S(1)}, f32[1,512]{1,0:T(1,128)}, u32[]{:S(2)}) copy-start(f32[1,512]{1,0:T(1,128)} %get-tuple-element.68) | copy-start | bytes 6148
  160.4 1.1 copy-start.5
  160.4 33.6 %copy-start.3 = (f32[6,128,512]{2,1,0:T(8,128)S(1)}, f32[6,128,512]{2,1,0:T(8,128)}, u32[]{:S(2)}) copy-start(f32[6,128,512]{2,1,0:T(8,128)} %get-tuple-element.62) | copy-start | bytes 4718596
  161.5 32.5 %collective-permute-start.1 = (f32[3,128,512]{2,1,0:T(8,128)S(1)}, f32[3,128,512]{2,1,0:T(8,128)S(1)}, u32[]{:S(2)}, u32[]{:S(2)}) collective-permute-start(f32[3,128,512]{2,1,0:T(8,128)S(1)} %copy-done.5), channel_id=1, source_target_pairs={{0,1},{1,0},{2,3},{3,2},{4,5},{5,4},{6,7},{7,6},{8,9},{9,8},{10,11... | collective-permute-start | bytes 2359304 | tf_op jit(solution)/shard_map/ppermute | solution.py:646
  194.1 261.2 %copy-start.4 = (f32[6,128,512]{2,1,0:T(8,128)}, f32[6,128,512]{2,1,0:T(8,128)S(1)}, u32[]{:S(2)}) copy-start(f32[6,128,512]{2,1,0:T(8,128)S(1)} %constant_dynamic-update-slice_fusion.2) | copy-start | bytes 4718596
  452.4 3.4 copy-start
Sparse Core Ops, SparseCore 0:
  160.5 288.7 all-reduce.2
